TPU v7x, 32 devices: a whole 2x2x4 slice. The times are simulated.
32 devices in a mesh: row: 4 (over y, x), col: 8 (over z, core).
Axes of the slice: x: 2, y: 2, z: 4, core: 2. Of those that a mesh axis runs over, the one named last changes fastest.
Arguments:
- points: int32 [16, 3, 1024], P('row', None, 'col'), may hold values from 0 to 31
- ranks: int32 [16], replicated, may hold values from 64 to 256, as said below
- bases: bfloat16 [16, 1024, 256], P('row', 'col'), may hold values from -0.375 to 0.375
- pivots: bfloat16 [2, 256, 256], replicated, may hold values from -0.119628906 to 0.119628906
- probes: bfloat16 [16, 64, 1024], P('col'), may hold values from -0.119628906 to 0.119628906
Outputs:
- updated: bfloat16 [16, 16, 256, 256], P('row', 'col')
- images: float32 [16, 64, 1024], P('row', None, 'col')
Inputs may be any that keep to these rules, and one draw needn't show every extreme that they name: `ranks`: the rank of each tile; some tile has rank 256 and some rank 256 // 4.
All inputs are finite; a program needn't handle non-finite values.
Results may differ from a plain program's by a relative error of at most 0.004.
The roundings to bfloat16 on the way count: a program that leaves them out, or rounds other values in their place, can miss the bound.
Values may be sent and summed in bfloat16 or wider, within the bound.
A program may use at most 64 MiB of HBM per device.

v0:
```python
import jax
import jax.numpy as jnp
from jax import lax
from jax.sharding import PartitionSpec as P

B = 1024
R = 256
PANELS = 2
nugget = 0.25
decay_length = 4.0
wave_length = 3.0


def spread(x, axis, root):
    mine = lax.axis_index(axis) == root
    return lax.psum(jnp.where(mine, x, jnp.zeros_like(x)), axis)


def kernel_block(rows, cols):
    diff = rows[:, :, None] - cols[:, None, :]
    dist = jnp.sqrt(jnp.sum(diff * diff, axis=0) + nugget)
    return (jnp.exp(-dist / decay_length) * jnp.cos(dist / wave_length)).astype(jnp.bfloat16)


def body(points, ranks, bases, pivots, probes):
    row_count = bases.shape[0]
    col_count = probes.shape[0]
    row_index = lax.axis_index("row")
    col_index = lax.axis_index("col")
    row_bases, row_points = (
        lax.all_gather(bases, "col", axis=1, tiled=True),
        lax.all_gather(points.astype(jnp.bfloat16), "col", axis=2, tiled=True),
    )
    root = col_index * col_count // row_count
    offset = col_index * col_count - root * row_count
    picked_bases = lax.dynamic_slice_in_dim(row_bases, offset, col_count, 0)
    picked_points = lax.dynamic_slice_in_dim(row_points, offset, col_count, 0)
    col_bases, col_points = (spread(picked_bases, "row", root), spread(picked_points, "row", root))
    col_coords = col_points.astype(jnp.float32)
    block = min(B, 256)
    nblocks = B // block

    def row_tile(item):
        tile_points, tile_bases = item
        coords = tile_points.astype(jnp.float32).reshape(3, nblocks, block).transpose(1, 0, 2)
        basis_blocks = tile_bases.reshape(nblocks, block, R)

        def add_block(total, blk):
            block_points, block_bases = blk
            tiles = jax.vmap(lambda other: kernel_block(block_points, other))(col_coords)
            proj = jnp.einsum(
                "jnm,jmr->jnr", tiles, col_bases, preferred_element_type=jnp.float32
            ).astype(jnp.bfloat16)
            return (
                total
                + jnp.einsum("nr,jns->jrs", block_bases, proj, preferred_element_type=jnp.float32),
                None,
            )

        total, _ = lax.scan(
            add_block, jnp.zeros((col_count, R, R), jnp.float32), (coords, basis_blocks)
        )
        return total

    raw = lax.map(row_tile, (row_points, row_bases))
    rank_iota = jnp.arange(R, dtype=jnp.int32)
    row_ranks = lax.dynamic_slice_in_dim(ranks, row_index * row_count, row_count)
    col_ranks = lax.dynamic_slice_in_dim(ranks, col_index * col_count, col_count)
    row_mask = (rank_iota[None, :] < row_ranks[:, None]).astype(jnp.float32)
    col_mask = (rank_iota[None, :] < col_ranks[:, None]).astype(jnp.float32)
    cores = (raw * row_mask[:, None, :, None] * col_mask[None, :, None, :]).astype(jnp.bfloat16)
    row_panel = spread(cores, "col", 0)
    col_panel = spread(cores[:PANELS], "row", 0)
    left = jnp.einsum(
        "ikab,kbc->ikac", row_panel, pivots, preferred_element_type=jnp.float32
    ).astype(jnp.bfloat16)
    update = jnp.einsum("ikac,kjcd->ijad", left, col_panel, preferred_element_type=jnp.float32)
    row_ids = row_index * row_count + jnp.arange(row_count, dtype=jnp.int32)
    col_ids = col_index * col_count + jnp.arange(col_count, dtype=jnp.int32)
    trailing = (row_ids >= PANELS)[:, None] & (col_ids >= PANELS)[None, :]
    updated = (
        cores.astype(jnp.float32) - jnp.where(trailing[:, :, None, None], update, 0.0)
    ).astype(jnp.bfloat16)
    probe_cores = jnp.einsum(
        "jpn,jnr->jpr", probes, col_bases, preferred_element_type=jnp.float32
    ).astype(jnp.bfloat16)
    partial_cores = jnp.einsum(
        "ijab,jpb->ipa", updated, probe_cores, preferred_element_type=jnp.float32
    )
    summed = lax.psum(partial_cores, "col")
    images = jnp.einsum(
        "ipa,ina->ipn", summed, bases.astype(jnp.float32), precision=lax.Precision.HIGHEST
    )
    return (updated, images)


def solution(mesh):
    placed = (P("row", None, "col"), P(), P("row", "col", None), P(), P("col", None, None))
    return jax.shard_map(
        body,
        mesh=mesh,
        in_specs=placed,
        out_specs=(P("row", "col", None, None), P("row", None, "col")),
        check_vma=False,
    )
```

profile of v0, /device:TPU:0, one launch (start us, length us, event | category | flops | bytes accessed | tf_op | source)
XLA Modules:
  0.0 444.0 jit_solution(3983174135087618088)
XLA Ops:
  7.2 0.7 all-gather.2.cloned.1.call-update
  8.0 33.5 %all-gather.2.cloned.1.call-done = bf16[4,1024,256]{2,1,0:T(8,128)(2,1)} async-done(((bf16[4,128,256]{2,1,0:T(8,128)(2,1)}), bf16[4,1024,256]{2,1,0:T(8,128)(2,1)}) %all-gather.2.cloned.1.call-update) | async-done | bytes 2097168 | tf_op jit(solution)/shard_map/all_gather | solution.py:31
  41.5 2.3 dynamic-slice_select_fusion
  43.9 10.4 %all_gather.6 = bf16[4,3,1024]{2,0,1:T(4,128)(2,1)S(1)} all-gather(bf16[4,3,128]{2,0,1:T(4,128)(2,1)S(1)} %convert_element_type.53), channel_id=1, replica_groups=mesh['row'=4,'col'=8] {'col'}, dimensions={2}, use_global_device_ids=true | all-gather | bytes 27648 | tf_op jit(solution)/shard_map/all_gather | solution.py:32
  54.3 16.0 %psum.35 = bf16[2,3,1024]{2,0,1:T(2,128)(2,1)S(1)} all-reduce(bf16[2,3,1024]{2,0,1:T(2,128)(2,1)S(1)} %broadcast_select_fusion.1), channel_id=1, replica_groups=mesh['row'=4,'col'=8] {'row'}, use_global_device_ids=true, to_apply=%region_0.1 | all-reduce | flops 6144 | bytes 24576 | tf_op jit(solution)/shard_map/psum | solution.py:16
  70.6 26.7 %all-reduce.5.cloned.1.call-done = bf16[2,1024,256]{2,1,0:T(8,128)(2,1)} async-done(((bf16[2,1024,256]{2,1,0:T(8,128)(2,1)}), bf16[2,1024,256]{2,1,0:T(8,128)(2,1)}) %all-reduce.5.cloned.1.call-update) | async-done | bytes 1048592 | tf_op jit(solution)/shard_map/psum | solution.py:16
  97.3 168.2 %while.25 = (s32[]{:T(128)}, f32[4,2,256,256]{3,2,1,0:T(8,128)}, bf16[4,3,1024]{2,1,0:T(4,128)(2,1)S(1)}, bf16[4,1024,256]{2,1,0:T(8,128)(2,1)}, f32[2,3,1024]{2...) while((s32[]{:T(128)}, f32[4,2,256,256]{3,2,1,0:T(8,128)}, ...), condition=%wide.region_6.7_spmd.clone, body=%wide.region_2.6_spmd.sunk.clone | while | flops 343280640 | bytes 9633548 | solution.py:65
  97.3 1.1 constant_dynamic-slice_fusion.7
  98.4 39.9 %while.24 = (s32[]{:T(128)}, f32[2,256,256]{1,2,0:T(8,128)S(1)}, f32[4,3,256]{2,1,0:T(4,128)S(1)}, f32[2,3,1024]{2,1,0:T(4,128)S(1)}, bf16[2,1024,256]{2,1,0:T(8...) while((s32[]{:T(128)}, f32[2,256,256]{1,2,0:T(8,128)S(1)}, ...), condition=%wide.region_5.5_spmd.clone, body=%wide.region_3.4_spmd.clone.sunk | while | flops 343277568 | bytes 6456423 | solution.py:60
  98.5 0.7 multiply_reduce_fusion.2
  99.1 9.3 %fusion.31 = f32[2,256,256]{1,2,0:T(8,128)S(1)} fusion(bf16[2,1024,256]{2,1,0:T(8,128)(2,1)} %get-tuple-element.269, f32[2,256,1024]{2,1,0:T(8,128)S(1)} %multiply_reduce_fusion.2, f32[2,256,256]{1,2,0:T(8,128)S(1)} %get-tuple-element.258, pred[]{:T(512)S(6)} %compare.5, bf16[4,256,256]{2,1,0:T(8,128)(2,1)S(1)} %get-tuple-element.270, ...), kind=kOutput, calls=%fused_computation.3.clone.1 | convolution fusion | flops 339083264 | bytes 4325381 | tf_op jit(solution)/shard_map/while/body/eval_jaxpr/while/body/eval_jaxpr/nr,jns->jrs/dot_general | solution.py:56
  108.4 0.7 multiply_reduce_fusion.2
  109.1 9.3 %fusion.31 = f32[2,256,256]{1,2,0:T(8,128)S(1)} fusion(bf16[2,1024,256]{2,1,0:T(8,128)(2,1)} %get-tuple-element.269, f32[2,256,1024]{2,1,0:T(8,128)S(1)} %multiply_reduce_fusion.2, f32[2,256,256]{1,2,0:T(8,128)S(1)} %get-tuple-element.258, pred[]{:T(512)S(6)} %compare.5, bf16[4,256,256]{2,1,0:T(8,128)(2,1)S(1)} %get-tuple-element.270, ...), kind=kOutput, calls=%fused_computation.3.clone.1 | convolution fusion | flops 339083264 | bytes 4325381 | tf_op jit(solution)/shard_map/while/body/eval_jaxpr/while/body/eval_jaxpr/nr,jns->jrs/dot_general | solution.py:56
  118.4 0.7 multiply_reduce_fusion.2
  119.1 9.3 %fusion.31 = f32[2,256,256]{1,2,0:T(8,128)S(1)} fusion(bf16[2,1024,256]{2,1,0:T(8,128)(2,1)} %get-tuple-element.269, f32[2,256,1024]{2,1,0:T(8,128)S(1)} %multiply_reduce_fusion.2, f32[2,256,256]{1,2,0:T(8,128)S(1)} %get-tuple-element.258, pred[]{:T(512)S(6)} %compare.5, bf16[4,256,256]{2,1,0:T(8,128)(2,1)S(1)} %get-tuple-element.270, ...), kind=kOutput, calls=%fused_computation.3.clone.1 | convolution fusion | flops 339083264 | bytes 4325381 | tf_op jit(solution)/shard_map/while/body/eval_jaxpr/while/body/eval_jaxpr/nr,jns->jrs/dot_general | solution.py:56
  128.4 0.7 multiply_reduce_fusion.2
  129.0 9.3 %fusion.31 = f32[2,256,256]{1,2,0:T(8,128)S(1)} fusion(bf16[2,1024,256]{2,1,0:T(8,128)(2,1)} %get-tuple-element.269, f32[2,256,1024]{2,1,0:T(8,128)S(1)} %multiply_reduce_fusion.2, f32[2,256,256]{1,2,0:T(8,128)S(1)} %get-tuple-element.258, pred[]{:T(512)S(6)} %compare.5, bf16[4,256,256]{2,1,0:T(8,128)(2,1)S(1)} %get-tuple-element.270, ...), kind=kOutput, calls=%fused_computation.3.clone.1 | convolution fusion | flops 339083264 | bytes 4325381 | tf_op jit(solution)/shard_map/while/body/eval_jaxpr/while/body/eval_jaxpr/nr,jns->jrs/dot_general | solution.py:56
  138.3 0.2 copy.34
  138.5 0.8 constant_dynamic-update-slice_fusion.3
  139.4 1.1 constant_dynamic-slice_fusion.7
  140.5 39.9 %while.24 = (s32[]{:T(128)}, f32[2,256,256]{1,2,0:T(8,128)S(1)}, f32[4,3,256]{2,1,0:T(4,128)S(1)}, f32[2,3,1024]{2,1,0:T(4,128)S(1)}, bf16[2,1024,256]{2,1,0:T(8...) while((s32[]{:T(128)}, f32[2,256,256]{1,2,0:T(8,128)S(1)}, ...), condition=%wide.region_5.5_spmd.clone, body=%wide.region_3.4_spmd.clone.sunk | while | flops 343277568 | bytes 6456423 | solution.py:60
  140.5 0.7 multiply_reduce_fusion.2
  141.2 9.3 %fusion.31 = f32[2,256,256]{1,2,0:T(8,128)S(1)} fusion(bf16[2,1024,256]{2,1,0:T(8,128)(2,1)} %get-tuple-element.269, f32[2,256,1024]{2,1,0:T(8,128)S(1)} %multiply_reduce_fusion.2, f32[2,256,256]{1,2,0:T(8,128)S(1)} %get-tuple-element.258, pred[]{:T(512)S(6)} %compare.5, bf16[4,256,256]{2,1,0:T(8,128)(2,1)S(1)} %get-tuple-element.270, ...), kind=kOutput, calls=%fused_computation.3.clone.1 | convolution fusion | flops 339083264 | bytes 4325381 | tf_op jit(solution)/shard_map/while/body/eval_jaxpr/while/body/eval_jaxpr/nr,jns->jrs/dot_general | solution.py:56
  150.5 0.7 multiply_reduce_fusion.2
  151.2 9.3 %fusion.31 = f32[2,256,256]{1,2,0:T(8,128)S(1)} fusion(bf16[2,1024,256]{2,1,0:T(8,128)(2,1)} %get-tuple-element.269, f32[2,256,1024]{2,1,0:T(8,128)S(1)} %multiply_reduce_fusion.2, f32[2,256,256]{1,2,0:T(8,128)S(1)} %get-tuple-element.258, pred[]{:T(512)S(6)} %compare.5, bf16[4,256,256]{2,1,0:T(8,128)(2,1)S(1)} %get-tuple-element.270, ...), kind=kOutput, calls=%fused_computation.3.clone.1 | convolution fusion | flops 339083264 | bytes 4325381 | tf_op jit(solution)/shard_map/while/body/eval_jaxpr/while/body/eval_jaxpr/nr,jns->jrs/dot_general | solution.py:56
  160.5 0.7 multiply_reduce_fusion.2
  161.1 9.3 %fusion.31 = f32[2,256,256]{1,2,0:T(8,128)S(1)} fusion(bf16[2,1024,256]{2,1,0:T(8,128)(2,1)} %get-tuple-element.269, f32[2,256,1024]{2,1,0:T(8,128)S(1)} %multiply_reduce_fusion.2, f32[2,256,256]{1,2,0:T(8,128)S(1)} %get-tuple-element.258, pred[]{:T(512)S(6)} %compare.5, bf16[4,256,256]{2,1,0:T(8,128)(2,1)S(1)} %get-tuple-element.270, ...), kind=kOutput, calls=%fused_computation.3.clone.1 | convolution fusion | flops 339083264 | bytes 4325381 | tf_op jit(solution)/shard_map/while/body/eval_jaxpr/while/body/eval_jaxpr/nr,jns->jrs/dot_general | solution.py:56
  170.4 0.7 multiply_reduce_fusion.2
  171.1 9.3 %fusion.31 = f32[2,256,256]{1,2,0:T(8,128)S(1)} fusion(bf16[2,1024,256]{2,1,0:T(8,128)(2,1)} %get-tuple-element.269, f32[2,256,1024]{2,1,0:T(8,128)S(1)} %multiply_reduce_fusion.2, f32[2,256,256]{1,2,0:T(8,128)S(1)} %get-tuple-element.258, pred[]{:T(512)S(6)} %compare.5, bf16[4,256,256]{2,1,0:T(8,128)(2,1)S(1)} %get-tuple-element.270, ...), kind=kOutput, calls=%fused_computation.3.clone.1 | convolution fusion | flops 339083264 | bytes 4325381 | tf_op jit(solution)/shard_map/while/body/eval_jaxpr/while/body/eval_jaxpr/nr,jns->jrs/dot_general | solution.py:56
  180.4 0.2 copy.34
  180.6 0.9 constant_dynamic-update-slice_fusion.3
  181.4 1.1 constant_dynamic-slice_fusion.7
  182.5 39.9 %while.24 = (s32[]{:T(128)}, f32[2,256,256]{1,2,0:T(8,128)S(1)}, f32[4,3,256]{2,1,0:T(4,128)S(1)}, f32[2,3,1024]{2,1,0:T(4,128)S(1)}, bf16[2,1024,256]{2,1,0:T(8...) while((s32[]{:T(128)}, f32[2,256,256]{1,2,0:T(8,128)S(1)}, ...), condition=%wide.region_5.5_spmd.clone, body=%wide.region_3.4_spmd.clone.sunk | while | flops 343277568 | bytes 6456423 | solution.py:60
  182.6 0.7 multiply_reduce_fusion.2
  183.2 9.3 %fusion.31 = f32[2,256,256]{1,2,0:T(8,128)S(1)} fusion(bf16[2,1024,256]{2,1,0:T(8,128)(2,1)} %get-tuple-element.269, f32[2,256,1024]{2,1,0:T(8,128)S(1)} %multiply_reduce_fusion.2, f32[2,256,256]{1,2,0:T(8,128)S(1)} %get-tuple-element.258, pred[]{:T(512)S(6)} %compare.5, bf16[4,256,256]{2,1,0:T(8,128)(2,1)S(1)} %get-tuple-element.270, ...), kind=kOutput, calls=%fused_computation.3.clone.1 | convolution fusion | flops 339083264 | bytes 4325381 | tf_op jit(solution)/shard_map/while/body/eval_jaxpr/while/body/eval_jaxpr/nr,jns->jrs/dot_general | solution.py:56
  192.5 0.7 multiply_reduce_fusion.2
  193.2 9.3 %fusion.31 = f32[2,256,256]{1,2,0:T(8,128)S(1)} fusion(bf16[2,1024,256]{2,1,0:T(8,128)(2,1)} %get-tuple-element.269, f32[2,256,1024]{2,1,0:T(8,128)S(1)} %multiply_reduce_fusion.2, f32[2,256,256]{1,2,0:T(8,128)S(1)} %get-tuple-element.258, pred[]{:T(512)S(6)} %compare.5, bf16[4,256,256]{2,1,0:T(8,128)(2,1)S(1)} %get-tuple-element.270, ...), kind=kOutput, calls=%fused_computation.3.clone.1 | convolution fusion | flops 339083264 | bytes 4325381 | tf_op jit(solution)/shard_map/while/body/eval_jaxpr/while/body/eval_jaxpr/nr,jns->jrs/dot_general | solution.py:56
  202.5 0.7 multiply_reduce_fusion.2
  203.2 9.3 %fusion.31 = f32[2,256,256]{1,2,0:T(8,128)S(1)} fusion(bf16[2,1024,256]{2,1,0:T(8,128)(2,1)} %get-tuple-element.269, f32[2,256,1024]{2,1,0:T(8,128)S(1)} %multiply_reduce_fusion.2, f32[2,256,256]{1,2,0:T(8,128)S(1)} %get-tuple-element.258, pred[]{:T(512)S(6)} %compare.5, bf16[4,256,256]{2,1,0:T(8,128)(2,1)S(1)} %get-tuple-element.270, ...), kind=kOutput, calls=%fused_computation.3.clone.1 | convolution fusion | flops 339083264 | bytes 4325381 | tf_op jit(solution)/shard_map/while/body/eval_jaxpr/while/body/eval_jaxpr/nr,jns->jrs/dot_general | solution.py:56
  212.5 0.7 multiply_reduce_fusion.2
  213.2 9.3 %fusion.31 = f32[2,256,256]{1,2,0:T(8,128)S(1)} fusion(bf16[2,1024,256]{2,1,0:T(8,128)(2,1)} %get-tuple-element.269, f32[2,256,1024]{2,1,0:T(8,128)S(1)} %multiply_reduce_fusion.2, f32[2,256,256]{1,2,0:T(8,128)S(1)} %get-tuple-element.258, pred[]{:T(512)S(6)} %compare.5, bf16[4,256,256]{2,1,0:T(8,128)(2,1)S(1)} %get-tuple-element.270, ...), kind=kOutput, calls=%fused_computation.3.clone.1 | convolution fusion | flops 339083264 | bytes 4325381 | tf_op jit(solution)/shard_map/while/body/eval_jaxpr/while/body/eval_jaxpr/nr,jns->jrs/dot_general | solution.py:56
  222.4 0.2 copy.34
  222.6 0.8 constant_dynamic-update-slice_fusion.3
  223.5 1.1 constant_dynamic-slice_fusion.7
  224.6 39.9 %while.24 = (s32[]{:T(128)}, f32[2,256,256]{1,2,0:T(8,128)S(1)}, f32[4,3,256]{2,1,0:T(4,128)S(1)}, f32[2,3,1024]{2,1,0:T(4,128)S(1)}, bf16[2,1024,256]{2,1,0:T(8...) while((s32[]{:T(128)}, f32[2,256,256]{1,2,0:T(8,128)S(1)}, ...), condition=%wide.region_5.5_spmd.clone, body=%wide.region_3.4_spmd.clone.sunk | while | flops 343277568 | bytes 6456423 | solution.py:60
  224.6 0.7 multiply_reduce_fusion.2
  225.3 9.3 %fusion.31 = f32[2,256,256]{1,2,0:T(8,128)S(1)} fusion(bf16[2,1024,256]{2,1,0:T(8,128)(2,1)} %get-tuple-element.269, f32[2,256,1024]{2,1,0:T(8,128)S(1)} %multiply_reduce_fusion.2, f32[2,256,256]{1,2,0:T(8,128)S(1)} %get-tuple-element.258, pred[]{:T(512)S(6)} %compare.5, bf16[4,256,256]{2,1,0:T(8,128)(2,1)S(1)} %get-tuple-element.270, ...), kind=kOutput, calls=%fused_computation.3.clone.1 | convolution fusion | flops 339083264 | bytes 4325381 | tf_op jit(solution)/shard_map/while/body/eval_jaxpr/while/body/eval_jaxpr/nr,jns->jrs/dot_general | solution.py:56
  234.6 0.7 multiply_reduce_fusion.2
  235.3 9.3 %fusion.31 = f32[2,256,256]{1,2,0:T(8,128)S(1)} fusion(bf16[2,1024,256]{2,1,0:T(8,128)(2,1)} %get-tuple-element.269, f32[2,256,1024]{2,1,0:T(8,128)S(1)} %multiply_reduce_fusion.2, f32[2,256,256]{1,2,0:T(8,128)S(1)} %get-tuple-element.258, pred[]{:T(512)S(6)} %compare.5, bf16[4,256,256]{2,1,0:T(8,128)(2,1)S(1)} %get-tuple-element.270, ...), kind=kOutput, calls=%fused_computation.3.clone.1 | convolution fusion | flops 339083264 | bytes 4325381 | tf_op jit(solution)/shard_map/while/body/eval_jaxpr/while/body/eval_jaxpr/nr,jns->jrs/dot_general | solution.py:56
  244.6 0.7 multiply_reduce_fusion.2
  245.2 9.3 %fusion.31 = f32[2,256,256]{1,2,0:T(8,128)S(1)} fusion(bf16[2,1024,256]{2,1,0:T(8,128)(2,1)} %get-tuple-element.269, f32[2,256,1024]{2,1,0:T(8,128)S(1)} %multiply_reduce_fusion.2, f32[2,256,256]{1,2,0:T(8,128)S(1)} %get-tuple-element.258, pred[]{:T(512)S(6)} %compare.5, bf16[4,256,256]{2,1,0:T(8,128)(2,1)S(1)} %get-tuple-element.270, ...), kind=kOutput, calls=%fused_computation.3.clone.1 | convolution fusion | flops 339083264 | bytes 4325381 | tf_op jit(solution)/shard_map/while/body/eval_jaxpr/while/body/eval_jaxpr/nr,jns->jrs/dot_general | solution.py:56
  254.5 0.7 multiply_reduce_fusion.2
  255.2 9.3 %fusion.31 = f32[2,256,256]{1,2,0:T(8,128)S(1)} fusion(bf16[2,1024,256]{2,1,0:T(8,128)(2,1)} %get-tuple-element.269, f32[2,256,1024]{2,1,0:T(8,128)S(1)} %multiply_reduce_fusion.2, f32[2,256,256]{1,2,0:T(8,128)S(1)} %get-tuple-element.258, pred[]{:T(512)S(6)} %compare.5, bf16[4,256,256]{2,1,0:T(8,128)(2,1)S(1)} %get-tuple-element.270, ...), kind=kOutput, calls=%fused_computation.3.clone.1 | convolution fusion | flops 339083264 | bytes 4325381 | tf_op jit(solution)/shard_map/while/body/eval_jaxpr/while/body/eval_jaxpr/nr,jns->jrs/dot_general | solution.py:56
  264.5 0.2 copy.34
  264.7 0.8 constant_dynamic-update-slice_fusion.3
  265.5 3.0 broadcast_select_fusion
  268.5 0.8 slice_select_fusion
  269.4 0.5 all-reduce.9.cloned.1.call-update
  270.1 44.8 %all-reduce.7.cloned.1.call-done = bf16[2,2,256,256]{3,2,1,0:T(8,128)(2,1)} async-done(((bf16[2,2,256,256]{3,2,1,0:T(8,128)(2,1)}), bf16[2,2,256,256]{3,2,1,0:T(8,128)(2,1)}) %all-reduce.7.cloned.1.call-update) | async-done | bytes 524304 | tf_op jit(solution)/shard_map/psum | solution.py:16
  314.8 61.6 %all-reduce.9.cloned.1.call-done = bf16[4,2,256,256]{3,2,1,0:T(8,128)(2,1)} async-done(((bf16[4,2,256,256]{3,2,1,0:T(8,128)(2,1)}), bf16[4,2,256,256]{3,2,1,0:T(8,128)(2,1)}) %all-reduce.9.cloned.1.call-update) | async-done | bytes 1048592 | tf_op jit(solution)/shard_map/psum | solution.py:16
  376.5 2.4 fusion.11
  378.9 2.6 convolution_bitcast_fusion.1
  381.5 54.0 %all-reduce.11.cloned.1.call-done = f32[4,64,256]{2,1,0:T(8,128)} async-done(((f32[4,64,256]{2,1,0:T(8,128)}), f32[4,64,256]{2,1,0:T(8,128)}) %all-reduce.11.cloned.1.call-update) | async-done | bytes 262160 | tf_op jit(solution)/shard_map/psum | solution.py:90
  435.5 2.0 fusion.18
  (60 shorter events, 0.9 us)
Async XLA Ops:
  7.2 369.3 %copy-start = (bf16[2,256,256]{2,1,0:T(8,128)(2,1)S(1)}, bf16[2,256,256]{2,1,0:T(8,128)(2,1)}, u32[]{:S(2)}) copy-start(bf16[2,256,256]{2,1,0:T(8,128)(2,1)} %param.12) | copy-start | bytes 786436
  7.2 36.7 %copy-start.4 = (s32[4,3,128]{2,0,1:T(4,128)S(1)}, s32[4,3,128]{2,0,1:T(4,128)}, u32[]{:S(2)}) copy-start(s32[4,3,128]{2,0,1:T(4,128)} %param.9) | copy-start | bytes 18436
  7.2 63.1 %copy-start.5 = (s32[16]{0:T(128)S(1)}, s32[16]{0:T(128)}, u32[]{:S(2)}) copy-start(s32[16]{0:T(128)} %param.10) | copy-start | bytes 196
  7.2 34.3 %all-gather.2.cloned.1.call-start = ((), (), s32[]{:S(2)}) async-start(), calls=%async_computation | async-start | bytes 2359296 | tf_op jit(solution)/shard_map/all_gather | solution.py:31
  7.9 89.4 %all-reduce.5.cloned.1.call-start = ((), (), s32[]{:S(2)}) async-start(), calls=%async_computation.1 | async-start | bytes 2097152 | tf_op jit(solution)/shard_map/psum | solution.py:16
  43.8 271.1 %all-reduce.7.cloned.1.call-start = ((), (), s32[]{:S(2)}) async-start(), calls=%async_computation.2 | async-start | bytes 1048576 | tf_op jit(solution)/shard_map/psum | solution.py:16
  269.3 107.1 %all-reduce.9.cloned.1.call-start = ((), (), s32[]{:S(2)}) async-start(), calls=%async_computation.3 | async-start | bytes 2097152 | tf_op jit(solution)/shard_map/psum | solution.py:16
  269.9 165.6 %all-reduce.11.cloned.1.call-start = ((), (), s32[]{:S(2)}) async-start(), calls=%async_computation.4 | async-start | bytes 524288 | tf_op jit(solution)/shard_map/psum | solution.py:90
  270.1 108.8 %copy-start.1 = (bf16[2,1024,256]{2,1,0:T(8,128)(2,1)S(1)}, bf16[2,1024,256]{2,1,0:T(8,128)(2,1)}, u32[]{:S(2)}) copy-start(bf16[2,1024,256]{2,1,0:T(8,128)(2,1)} %get-tuple-element.313) | copy-start | bytes 3145732
  378.9 58.6 %copy-start.2 = (bf16[4,2,256,256]{3,2,1,0:T(8,128)(2,1)}, bf16[4,2,256,256]{3,2,1,0:T(8,128)(2,1)S(1)}, u32[]{:S(2)}) copy-start(bf16[4,2,256,256]{3,2,1,0:T(8,128)(2,1)S(1)} %fusion.11) | copy-start | bytes 3145732
  378.9 56.6 %copy-start.3 = (bf16[4,128,256]{2,1,0:T(8,128)(2,1)S(1)}, bf16[4,128,256]{2,1,0:T(8,128)(2,1)}, u32[]{:S(2)}) copy-start(bf16[4,128,256]{2,1,0:T(8,128)(2,1)} %param.11) | copy-start | bytes 786436
Sparse Core Ops, SparseCore 0:
  9.6 31.7 all-gather.1
  45.1 52.1 all-reduce.4
  269.5 45.3 all-reduce.6
  317.6 58.8 all-reduce.8
  381.6 53.8 all-reduce.10
where the time goes:
time: 445 us; the launch traced here: 444 us
  waiting for transfers between devices  222 us (50%)
  matrix products  155 us (35%)
  blocking collectives  26.4 us (6%)
  other arithmetic  16.8 us (4%)
  between operations  13.9 us (3%)
  local copies, waits for them, and re-layouts  8.84 us (2%)
    dot_general x16, matrix products, add_block(): jnp.einsum('nr,jns->jrs', block_bases, proj, preferred_element_type=jnp.f...  148 us
    psum x3, waiting for transfers between devices, spread(): return lax.psum(jnp.where(mine, x, jnp.zeros_like(x)), axis)  133 us
    psum x1, waiting for transfers between devices, body(): summed = lax.psum(partial_cores, 'col')  54 us
    all_gather x1, waiting for transfers between devices, body(): lax.all_gather(bases, 'col', axis=1, tiled=True)  33.5 us
    psum x1, blocking collectives, spread(): return lax.psum(jnp.where(mine, x, jnp.zeros_like(x)), axis)  16 us
    reduce_sum x16, other arithmetic, kernel_block(): dist = jnp.sqrt(jnp.sum(diff * diff, axis=0) + nugget)  10.5 us
    all_gather x1, blocking collectives, body(): lax.all_gather(points.astype(jnp.bfloat16), 'col', axis=2, tiled=True)  10.4 us
  transfers between devices with their start and end apart: 5, of which 5 were waited for; matrix products, arithmetic and copies ran while one was open for 0% of the time, Pallas kernels for 0%

commit v1 on v0

--- a/solution.py
+++ b/solution.py
@@ -87,7 +87,9 @@
     partial_cores = jnp.einsum(
         "ijab,jpb->ipa", updated, probe_cores, preferred_element_type=jnp.float32
     )
-    summed = lax.psum(partial_cores, "col")
+    summed = partial_cores
+    for hop in (1, 2, 4):
+        summed = summed + lax.ppermute(summed, "col", [(dev, dev ^ hop) for dev in range(8)])
     images = jnp.einsum(
         "ipa,ina->ipn", summed, bases.astype(jnp.float32), precision=lax.Precision.HIGHEST
     )

time: 445 us -> 414 us (0.930)
  waiting for transfers between devices: 222 us -> 190 us
    psum x1 -> x0, waiting for transfers between devices: 54 us -> none  [body(): summed = lax.psum(partial_cores, 'col')]
    ppermute x0 -> x3, waiting for transfers between devices: none -> 21.9 us  [body(): lax.ppermute(summed, 'col', [(dev, dev ^ hop) for dev in range(8)])]
  transfers between devices with their start and end apart: 5 -> 7, of which waited for: 5 -> 7; matrix products, arithmetic and copies ran while one was open for 0% -> 0% of each run, Pallas kernels for 0% -> 0%
where the time goes in v1:
time: 414 us; the launch traced here: 413 us
  waiting for transfers between devices  190 us (46%)
  matrix products  154 us (37%)
  blocking collectives  26.4 us (6%)
  other arithmetic  16.9 us (4%)
  between operations  13.9 us (3%)
  local copies, waits for them, and re-layouts  8.82 us (2%)
    dot_general x16, matrix products, add_block(): jnp.einsum('nr,jns->jrs', block_bases, proj, preferred_element_type=jnp.f...  148 us
    psum x3, waiting for transfers between devices, spread(): return lax.psum(jnp.where(mine, x, jnp.zeros_like(x)), axis)  133 us
    all_gather x1, waiting for transfers between devices, body(): lax.all_gather(bases, 'col', axis=1, tiled=True)  33.5 us
    ppermute x3, waiting for transfers between devices, body(): lax.ppermute(summed, 'col', [(dev, dev ^ hop) for dev in range(8)])  21.9 us
    psum x1, blocking collectives, spread(): return lax.psum(jnp.where(mine, x, jnp.zeros_like(x)), axis)  16 us
    reduce_sum x16, other arithmetic, kernel_block(): dist = jnp.sqrt(jnp.sum(diff * diff, axis=0) + nugget)  10.5 us
    all_gather x1, blocking collectives, body(): lax.all_gather(points.astype(jnp.bfloat16), 'col', axis=2, tiled=True)  10.4 us
  transfers between devices with their start and end apart: 7, of which 7 were waited for; matrix products, arithmetic and copies ran while one was open for 0% of the time, Pallas kernels for 0%

profile of v1, /device:TPU:0, one launch (start us, length us, event | category | flops | bytes accessed | tf_op | source)
XLA Modules:
  0.0 412.5 jit_solution(17436371730478413459)
XLA Ops:
  7.2 0.7 all-gather.2.cloned.1.call-update
  8.0 33.5 %all-gather.2.cloned.1.call-done = bf16[4,1024,256]{2,1,0:T(8,128)(2,1)} async-done(((bf16[4,128,256]{2,1,0:T(8,128)(2,1)}), bf16[4,1024,256]{2,1,0:T(8,128)(2,1)}) %all-gather.2.cloned.1.call-update) | async-done | bytes 2097168 | tf_op jit(solution)/shard_map/all_gather | solution.py:31
  41.5 2.3 dynamic-slice_select_fusion
  43.9 10.4 %all_gather.6 = bf16[4,3,1024]{2,0,1:T(4,128)(2,1)S(1)} all-gather(bf16[4,3,128]{2,0,1:T(4,128)(2,1)S(1)} %convert_element_type.53), channel_id=1, replica_groups=mesh['row'=4,'col'=8] {'col'}, dimensions={2}, use_global_device_ids=true | all-gather | bytes 27648 | tf_op jit(solution)/shard_map/all_gather | solution.py:32
  54.3 16.0 %psum.28 = bf16[2,3,1024]{2,0,1:T(2,128)(2,1)S(1)} all-reduce(bf16[2,3,1024]{2,0,1:T(2,128)(2,1)S(1)} %broadcast_select_fusion.1), channel_id=1, replica_groups=mesh['row'=4,'col'=8] {'row'}, use_global_device_ids=true, to_apply=%region_0.1 | all-reduce | flops 6144 | bytes 24576 | tf_op jit(solution)/shard_map/psum | solution.py:16
  70.6 26.7 %all-reduce.4.cloned.1.call-done = bf16[2,1024,256]{2,1,0:T(8,128)(2,1)} async-done(((bf16[2,1024,256]{2,1,0:T(8,128)(2,1)}), bf16[2,1024,256]{2,1,0:T(8,128)(2,1)}) %all-reduce.4.cloned.1.call-update) | async-done | bytes 1048592 | tf_op jit(solution)/shard_map/psum | solution.py:16
  97.3 168.2 %while.25 = (s32[]{:T(128)}, f32[4,2,256,256]{3,2,1,0:T(8,128)}, bf16[4,3,1024]{2,1,0:T(4,128)(2,1)S(1)}, bf16[4,1024,256]{2,1,0:T(8,128)(2,1)}, f32[2,3,1024]{2...) while((s32[]{:T(128)}, f32[4,2,256,256]{3,2,1,0:T(8,128)}, ...), condition=%wide.region_6.7_spmd.clone, body=%wide.region_2.6_spmd.sunk.clone | while | flops 343280640 | bytes 9633548 | solution.py:65
  97.3 1.1 constant_dynamic-slice_fusion.7
  98.4 39.9 %while.24 = (s32[]{:T(128)}, f32[2,256,256]{1,2,0:T(8,128)S(1)}, f32[4,3,256]{2,1,0:T(4,128)S(1)}, f32[2,3,1024]{2,1,0:T(4,128)S(1)}, bf16[2,1024,256]{2,1,0:T(8...) while((s32[]{:T(128)}, f32[2,256,256]{1,2,0:T(8,128)S(1)}, ...), condition=%wide.region_5.5_spmd.clone, body=%wide.region_3.4_spmd.clone.sunk | while | flops 343277568 | bytes 6456423 | solution.py:60
  98.5 0.7 multiply_reduce_fusion.2
  99.1 9.3 %fusion.31 = f32[2,256,256]{1,2,0:T(8,128)S(1)} fusion(bf16[2,1024,256]{2,1,0:T(8,128)(2,1)} %get-tuple-element.269, f32[2,256,1024]{2,1,0:T(8,128)S(1)} %multiply_reduce_fusion.2, f32[2,256,256]{1,2,0:T(8,128)S(1)} %get-tuple-element.258, pred[]{:T(512)S(6)} %compare.5, bf16[4,256,256]{2,1,0:T(8,128)(2,1)S(1)} %get-tuple-element.270, ...), kind=kOutput, calls=%fused_computation.3.clone.1 | convolution fusion | flops 339083264 | bytes 4325381 | tf_op jit(solution)/shard_map/while/body/eval_jaxpr/while/body/eval_jaxpr/nr,jns->jrs/dot_general | solution.py:56
  108.4 0.7 multiply_reduce_fusion.2
  109.1 9.3 %fusion.31 = f32[2,256,256]{1,2,0:T(8,128)S(1)} fusion(bf16[2,1024,256]{2,1,0:T(8,128)(2,1)} %get-tuple-element.269, f32[2,256,1024]{2,1,0:T(8,128)S(1)} %multiply_reduce_fusion.2, f32[2,256,256]{1,2,0:T(8,128)S(1)} %get-tuple-element.258, pred[]{:T(512)S(6)} %compare.5, bf16[4,256,256]{2,1,0:T(8,128)(2,1)S(1)} %get-tuple-element.270, ...), kind=kOutput, calls=%fused_computation.3.clone.1 | convolution fusion | flops 339083264 | bytes 4325381 | tf_op jit(solution)/shard_map/while/body/eval_jaxpr/while/body/eval_jaxpr/nr,jns->jrs/dot_general | solution.py:56
  118.4 0.7 multiply_reduce_fusion.2
  119.1 9.3 %fusion.31 = f32[2,256,256]{1,2,0:T(8,128)S(1)} fusion(bf16[2,1024,256]{2,1,0:T(8,128)(2,1)} %get-tuple-element.269, f32[2,256,1024]{2,1,0:T(8,128)S(1)} %multiply_reduce_fusion.2, f32[2,256,256]{1,2,0:T(8,128)S(1)} %get-tuple-element.258, pred[]{:T(512)S(6)} %compare.5, bf16[4,256,256]{2,1,0:T(8,128)(2,1)S(1)} %get-tuple-element.270, ...), kind=kOutput, calls=%fused_computation.3.clone.1 | convolution fusion | flops 339083264 | bytes 4325381 | tf_op jit(solution)/shard_map/while/body/eval_jaxpr/while/body/eval_jaxpr/nr,jns->jrs/dot_general | solution.py:56
  128.4 0.7 multiply_reduce_fusion.2
  129.1 9.3 %fusion.31 = f32[2,256,256]{1,2,0:T(8,128)S(1)} fusion(bf16[2,1024,256]{2,1,0:T(8,128)(2,1)} %get-tuple-element.269, f32[2,256,1024]{2,1,0:T(8,128)S(1)} %multiply_reduce_fusion.2, f32[2,256,256]{1,2,0:T(8,128)S(1)} %get-tuple-element.258, pred[]{:T(512)S(6)} %compare.5, bf16[4,256,256]{2,1,0:T(8,128)(2,1)S(1)} %get-tuple-element.270, ...), kind=kOutput, calls=%fused_computation.3.clone.1 | convolution fusion | flops 339083264 | bytes 4325381 | tf_op jit(solution)/shard_map/while/body/eval_jaxpr/while/body/eval_jaxpr/nr,jns->jrs/dot_general | solution.py:56
  138.5 0.8 constant_dynamic-update-slice_fusion.3
  139.4 1.1 constant_dynamic-slice_fusion.7
  140.5 39.9 %while.24 = (s32[]{:T(128)}, f32[2,256,256]{1,2,0:T(8,128)S(1)}, f32[4,3,256]{2,1,0:T(4,128)S(1)}, f32[2,3,1024]{2,1,0:T(4,128)S(1)}, bf16[2,1024,256]{2,1,0:T(8...) while((s32[]{:T(128)}, f32[2,256,256]{1,2,0:T(8,128)S(1)}, ...), condition=%wide.region_5.5_spmd.clone, body=%wide.region_3.4_spmd.clone.sunk | while | flops 343277568 | bytes 6456423 | solution.py:60
  140.5 0.7 multiply_reduce_fusion.2
  141.2 9.3 %fusion.31 = f32[2,256,256]{1,2,0:T(8,128)S(1)} fusion(bf16[2,1024,256]{2,1,0:T(8,128)(2,1)} %get-tuple-element.269, f32[2,256,1024]{2,1,0:T(8,128)S(1)} %multiply_reduce_fusion.2, f32[2,256,256]{1,2,0:T(8,128)S(1)} %get-tuple-element.258, pred[]{:T(512)S(6)} %compare.5, bf16[4,256,256]{2,1,0:T(8,128)(2,1)S(1)} %get-tuple-element.270, ...), kind=kOutput, calls=%fused_computation.3.clone.1 | convolution fusion | flops 339083264 | bytes 4325381 | tf_op jit(solution)/shard_map/while/body/eval_jaxpr/while/body/eval_jaxpr/nr,jns->jrs/dot_general | solution.py:56
  150.5 0.7 multiply_reduce_fusion.2
  151.2 9.3 %fusion.31 = f32[2,256,256]{1,2,0:T(8,128)S(1)} fusion(bf16[2,1024,256]{2,1,0:T(8,128)(2,1)} %get-tuple-element.269, f32[2,256,1024]{2,1,0:T(8,128)S(1)} %multiply_reduce_fusion.2, f32[2,256,256]{1,2,0:T(8,128)S(1)} %get-tuple-element.258, pred[]{:T(512)S(6)} %compare.5, bf16[4,256,256]{2,1,0:T(8,128)(2,1)S(1)} %get-tuple-element.270, ...), kind=kOutput, calls=%fused_computation.3.clone.1 | convolution fusion | flops 339083264 | bytes 4325381 | tf_op jit(solution)/shard_map/while/body/eval_jaxpr/while/body/eval_jaxpr/nr,jns->jrs/dot_general | solution.py:56
  160.5 0.7 multiply_reduce_fusion.2
  161.2 9.3 %fusion.31 = f32[2,256,256]{1,2,0:T(8,128)S(1)} fusion(bf16[2,1024,256]{2,1,0:T(8,128)(2,1)} %get-tuple-element.269, f32[2,256,1024]{2,1,0:T(8,128)S(1)} %multiply_reduce_fusion.2, f32[2,256,256]{1,2,0:T(8,128)S(1)} %get-tuple-element.258, pred[]{:T(512)S(6)} %compare.5, bf16[4,256,256]{2,1,0:T(8,128)(2,1)S(1)} %get-tuple-element.270, ...), kind=kOutput, calls=%fused_computation.3.clone.1 | convolution fusion | flops 339083264 | bytes 4325381 | tf_op jit(solution)/shard_map/while/body/eval_jaxpr/while/body/eval_jaxpr/nr,jns->jrs/dot_general | solution.py:56
  170.5 0.7 multiply_reduce_fusion.2
  171.1 9.3 %fusion.31 = f32[2,256,256]{1,2,0:T(8,128)S(1)} fusion(bf16[2,1024,256]{2,1,0:T(8,128)(2,1)} %get-tuple-element.269, f32[2,256,1024]{2,1,0:T(8,128)S(1)} %multiply_reduce_fusion.2, f32[2,256,256]{1,2,0:T(8,128)S(1)} %get-tuple-element.258, pred[]{:T(512)S(6)} %compare.5, bf16[4,256,256]{2,1,0:T(8,128)(2,1)S(1)} %get-tuple-element.270, ...), kind=kOutput, calls=%fused_computation.3.clone.1 | convolution fusion | flops 339083264 | bytes 4325381 | tf_op jit(solution)/shard_map/while/body/eval_jaxpr/while/body/eval_jaxpr/nr,jns->jrs/dot_general | solution.py:56
  180.6 0.8 constant_dynamic-update-slice_fusion.3
  181.5 1.1 constant_dynamic-slice_fusion.7
  182.6 39.9 %while.24 = (s32[]{:T(128)}, f32[2,256,256]{1,2,0:T(8,128)S(1)}, f32[4,3,256]{2,1,0:T(4,128)S(1)}, f32[2,3,1024]{2,1,0:T(4,128)S(1)}, bf16[2,1024,256]{2,1,0:T(8...) while((s32[]{:T(128)}, f32[2,256,256]{1,2,0:T(8,128)S(1)}, ...), condition=%wide.region_5.5_spmd.clone, body=%wide.region_3.4_spmd.clone.sunk | while | flops 343277568 | bytes 6456423 | solution.py:60
  182.6 0.7 multiply_reduce_fusion.2
  183.3 9.3 %fusion.31 = f32[2,256,256]{1,2,0:T(8,128)S(1)} fusion(bf16[2,1024,256]{2,1,0:T(8,128)(2,1)} %get-tuple-element.269, f32[2,256,1024]{2,1,0:T(8,128)S(1)} %multiply_reduce_fusion.2, f32[2,256,256]{1,2,0:T(8,128)S(1)} %get-tuple-element.258, pred[]{:T(512)S(6)} %compare.5, bf16[4,256,256]{2,1,0:T(8,128)(2,1)S(1)} %get-tuple-element.270, ...), kind=kOutput, calls=%fused_computation.3.clone.1 | convolution fusion | flops 339083264 | bytes 4325381 | tf_op jit(solution)/shard_map/while/body/eval_jaxpr/while/body/eval_jaxpr/nr,jns->jrs/dot_general | solution.py:56
  192.6 0.7 multiply_reduce_fusion.2
  193.2 9.3 %fusion.31 = f32[2,256,256]{1,2,0:T(8,128)S(1)} fusion(bf16[2,1024,256]{2,1,0:T(8,128)(2,1)} %get-tuple-element.269, f32[2,256,1024]{2,1,0:T(8,128)S(1)} %multiply_reduce_fusion.2, f32[2,256,256]{1,2,0:T(8,128)S(1)} %get-tuple-element.258, pred[]{:T(512)S(6)} %compare.5, bf16[4,256,256]{2,1,0:T(8,128)(2,1)S(1)} %get-tuple-element.270, ...), kind=kOutput, calls=%fused_computation.3.clone.1 | convolution fusion | flops 339083264 | bytes 4325381 | tf_op jit(solution)/shard_map/while/body/eval_jaxpr/while/body/eval_jaxpr/nr,jns->jrs/dot_general | solution.py:56
  202.5 0.7 multiply_reduce_fusion.2
  203.2 9.3 %fusion.31 = f32[2,256,256]{1,2,0:T(8,128)S(1)} fusion(bf16[2,1024,256]{2,1,0:T(8,128)(2,1)} %get-tuple-element.269, f32[2,256,1024]{2,1,0:T(8,128)S(1)} %multiply_reduce_fusion.2, f32[2,256,256]{1,2,0:T(8,128)S(1)} %get-tuple-element.258, pred[]{:T(512)S(6)} %compare.5, bf16[4,256,256]{2,1,0:T(8,128)(2,1)S(1)} %get-tuple-element.270, ...), kind=kOutput, calls=%fused_computation.3.clone.1 | convolution fusion | flops 339083264 | bytes 4325381 | tf_op jit(solution)/shard_map/while/body/eval_jaxpr/while/body/eval_jaxpr/nr,jns->jrs/dot_general | solution.py:56
  212.5 0.7 multiply_reduce_fusion.2
  213.2 9.3 %fusion.31 = f32[2,256,256]{1,2,0:T(8,128)S(1)} fusion(bf16[2,1024,256]{2,1,0:T(8,128)(2,1)} %get-tuple-element.269, f32[2,256,1024]{2,1,0:T(8,128)S(1)} %multiply_reduce_fusion.2, f32[2,256,256]{1,2,0:T(8,128)S(1)} %get-tuple-element.258, pred[]{:T(512)S(6)} %compare.5, bf16[4,256,256]{2,1,0:T(8,128)(2,1)S(1)} %get-tuple-element.270, ...), kind=kOutput, calls=%fused_computation.3.clone.1 | convolution fusion | flops 339083264 | bytes 4325381 | tf_op jit(solution)/shard_map/while/body/eval_jaxpr/while/body/eval_jaxpr/nr,jns->jrs/dot_general | solution.py:56
  222.7 0.8 constant_dynamic-update-slice_fusion.3
  223.5 1.1 constant_dynamic-slice_fusion.7
  224.6 39.9 %while.24 = (s32[]{:T(128)}, f32[2,256,256]{1,2,0:T(8,128)S(1)}, f32[4,3,256]{2,1,0:T(4,128)S(1)}, f32[2,3,1024]{2,1,0:T(4,128)S(1)}, bf16[2,1024,256]{2,1,0:T(8...) while((s32[]{:T(128)}, f32[2,256,256]{1,2,0:T(8,128)S(1)}, ...), condition=%wide.region_5.5_spmd.clone, body=%wide.region_3.4_spmd.clone.sunk | while | flops 343277568 | bytes 6456423 | solution.py:60
  224.7 0.7 multiply_reduce_fusion.2
  225.3 9.3 %fusion.31 = f32[2,256,256]{1,2,0:T(8,128)S(1)} fusion(bf16[2,1024,256]{2,1,0:T(8,128)(2,1)} %get-tuple-element.269, f32[2,256,1024]{2,1,0:T(8,128)S(1)} %multiply_reduce_fusion.2, f32[2,256,256]{1,2,0:T(8,128)S(1)} %get-tuple-element.258, pred[]{:T(512)S(6)} %compare.5, bf16[4,256,256]{2,1,0:T(8,128)(2,1)S(1)} %get-tuple-element.270, ...), kind=kOutput, calls=%fused_computation.3.clone.1 | convolution fusion | flops 339083264 | bytes 4325381 | tf_op jit(solution)/shard_map/while/body/eval_jaxpr/while/body/eval_jaxpr/nr,jns->jrs/dot_general | solution.py:56
  234.6 0.7 multiply_reduce_fusion.2
  235.3 9.3 %fusion.31 = f32[2,256,256]{1,2,0:T(8,128)S(1)} fusion(bf16[2,1024,256]{2,1,0:T(8,128)(2,1)} %get-tuple-element.269, f32[2,256,1024]{2,1,0:T(8,128)S(1)} %multiply_reduce_fusion.2, f32[2,256,256]{1,2,0:T(8,128)S(1)} %get-tuple-element.258, pred[]{:T(512)S(6)} %compare.5, bf16[4,256,256]{2,1,0:T(8,128)(2,1)S(1)} %get-tuple-element.270, ...), kind=kOutput, calls=%fused_computation.3.clone.1 | convolution fusion | flops 339083264 | bytes 4325381 | tf_op jit(solution)/shard_map/while/body/eval_jaxpr/while/body/eval_jaxpr/nr,jns->jrs/dot_general | solution.py:56
  244.6 0.7 multiply_reduce_fusion.2
  245.3 9.3 %fusion.31 = f32[2,256,256]{1,2,0:T(8,128)S(1)} fusion(bf16[2,1024,256]{2,1,0:T(8,128)(2,1)} %get-tuple-element.269, f32[2,256,1024]{2,1,0:T(8,128)S(1)} %multiply_reduce_fusion.2, f32[2,256,256]{1,2,0:T(8,128)S(1)} %get-tuple-element.258, pred[]{:T(512)S(6)} %compare.5, bf16[4,256,256]{2,1,0:T(8,128)(2,1)S(1)} %get-tuple-element.270, ...), kind=kOutput, calls=%fused_computation.3.clone.1 | convolution fusion | flops 339083264 | bytes 4325381 | tf_op jit(solution)/shard_map/while/body/eval_jaxpr/while/body/eval_jaxpr/nr,jns->jrs/dot_general | solution.py:56
  254.6 0.7 multiply_reduce_fusion.2
  255.2 9.3 %fusion.31 = f32[2,256,256]{1,2,0:T(8,128)S(1)} fusion(bf16[2,1024,256]{2,1,0:T(8,128)(2,1)} %get-tuple-element.269, f32[2,256,1024]{2,1,0:T(8,128)S(1)} %multiply_reduce_fusion.2, f32[2,256,256]{1,2,0:T(8,128)S(1)} %get-tuple-element.258, pred[]{:T(512)S(6)} %compare.5, bf16[4,256,256]{2,1,0:T(8,128)(2,1)S(1)} %get-tuple-element.270, ...), kind=kOutput, calls=%fused_computation.3.clone.1 | convolution fusion | flops 339083264 | bytes 4325381 | tf_op jit(solution)/shard_map/while/body/eval_jaxpr/while/body/eval_jaxpr/nr,jns->jrs/dot_general | solution.py:56
  264.7 0.8 constant_dynamic-update-slice_fusion.3
  265.6 2.9 broadcast_select_fusion
  268.5 0.8 slice_select_fusion
  269.4 0.5 all-reduce.8.cloned.1.call-update
  270.0 44.8 %all-reduce.6.cloned.1.call-done = bf16[2,2,256,256]{3,2,1,0:T(8,128)(2,1)} async-done(((bf16[2,2,256,256]{3,2,1,0:T(8,128)(2,1)}), bf16[2,2,256,256]{3,2,1,0:T(8,128)(2,1)}) %all-reduce.6.cloned.1.call-update) | async-done | bytes 524304 | tf_op jit(solution)/shard_map/psum | solution.py:16
  314.8 61.6 %all-reduce.8.cloned.1.call-done = bf16[4,2,256,256]{3,2,1,0:T(8,128)(2,1)} async-done(((bf16[4,2,256,256]{3,2,1,0:T(8,128)(2,1)}), bf16[4,2,256,256]{3,2,1,0:T(8,128)(2,1)}) %all-reduce.8.cloned.1.call-update) | async-done | bytes 1048592 | tf_op jit(solution)/shard_map/psum | solution.py:16
  376.5 2.4 fusion.11
  378.9 1.9 convolution_bitcast_fusion.1
  380.8 1.5 collective-permute-done
  382.4 0.7 collective-permute-start.1
  383.1 7.7 %collective-permute-done.1 = f32[4,64,256]{2,1,0:T(8,128)S(1)} collective-permute-done((f32[4,64,256]{2,1,0:T(8,128)S(1)}, f32[4,64,256]{2,1,0:T(8,128)S(1)}, u32[]{:S(2)}, u32[]{:S(2)}) %collective-permute-start.1) | collective-permute-done | bytes 262176 | tf_op jit(solution)/shard_map/ppermute | solution.py:92
  390.8 1.4 collective-permute-start.2
  392.3 12.7 %collective-permute-done.2 = f32[4,64,256]{2,1,0:T(8,128)S(1)} collective-permute-done((f32[4,64,256]{2,1,0:T(8,128)S(1)}, f32[4,64,256]{2,1,0:T(8,128)S(1)}, u32[]{:S(2)}, u32[]{:S(2)}) %collective-permute-start.2) | collective-permute-done | bytes 262176 | tf_op jit(solution)/shard_map/ppermute | solution.py:92
  404.9 1.1 fusion.17
  (65 shorter events, 1.8 us)
Async XLA Ops:
  7.2 369.3 %copy-start = (bf16[2,256,256]{2,1,0:T(8,128)(2,1)S(1)}, bf16[2,256,256]{2,1,0:T(8,128)(2,1)}, u32[]{:S(2)}) copy-start(bf16[2,256,256]{2,1,0:T(8,128)(2,1)} %param.12) | copy-start | bytes 786436
  7.2 36.7 %copy-start.4 = (s32[4,3,128]{2,0,1:T(4,128)S(1)}, s32[4,3,128]{2,0,1:T(4,128)}, u32[]{:S(2)}) copy-start(s32[4,3,128]{2,0,1:T(4,128)} %param.9) | copy-start | bytes 18436
  7.2 63.1 %copy-start.5 = (s32[16]{0:T(128)S(1)}, s32[16]{0:T(128)}, u32[]{:S(2)}) copy-start(s32[16]{0:T(128)} %param.10) | copy-start | bytes 196
  7.2 34.3 %all-gather.2.cloned.1.call-start = ((), (), s32[]{:S(2)}) async-start(), calls=%async_computation | async-start | bytes 2359296 | tf_op jit(solution)/shard_map/all_gather | solution.py:31
  7.9 89.4 %all-reduce.4.cloned.1.call-start = ((), (), s32[]{:S(2)}) async-start(), calls=%async_computation.1 | async-start | bytes 2097152 | tf_op jit(solution)/shard_map/psum | solution.py:16
  43.8 271.0 %all-reduce.6.cloned.1.call-start = ((), (), s32[]{:S(2)}) async-start(), calls=%async_computation.2 | async-start | bytes 1048576 | tf_op jit(solution)/shard_map/psum | solution.py:16
  269.3 107.1 %all-reduce.8.cloned.1.call-start = ((), (), s32[]{:S(2)}) async-start(), calls=%async_computation.3 | async-start | bytes 2097152 | tf_op jit(solution)/shard_map/psum | solution.py:16
  270.0 108.8 %copy-start.2 = (bf16[2,1024,256]{2,1,0:T(8,128)(2,1)S(1)}, bf16[2,1024,256]{2,1,0:T(8,128)(2,1)}, u32[]{:S(2)}) copy-start(bf16[2,1024,256]{2,1,0:T(8,128)(2,1)} %get-tuple-element.315) | copy-start | bytes 3145732
  378.9 27.1 %copy-start.3 = (bf16[4,2,256,256]{3,2,1,0:T(8,128)(2,1)}, bf16[4,2,256,256]{3,2,1,0:T(8,128)(2,1)S(1)}, u32[]{:S(2)}) copy-start(bf16[4,2,256,256]{3,2,1,0:T(8,128)(2,1)S(1)} %fusion.11) | copy-start | bytes 3145732
  378.9 26.1 %copy-start.1 = (bf16[4,128,256]{2,1,0:T(8,128)(2,1)S(1)}, bf16[4,128,256]{2,1,0:T(8,128)(2,1)}, u32[]{:S(2)}) copy-start(bf16[4,128,256]{2,1,0:T(8,128)(2,1)} %param.11) | copy-start | bytes 786436
  380.7 1.6 collective-permute-start
  382.4 8.4 %collective-permute-start.1 = (f32[4,64,256]{2,1,0:T(8,128)S(1)}, f32[4,64,256]{2,1,0:T(8,128)S(1)}, u32[]{:S(2)}, u32[]{:S(2)}) collective-permute-start(f32[4,64,256]{2,1,0:T(8,128)S(1)} %add.67), channel_id=1, source_target_pairs={{0,2},{1,3},{2,0},{3,1},{4,6},{5,7},{6,4},{7,5},{8,10},{9,11},{10,... | collective-permute-start | bytes 786440 | tf_op jit(solution)/shard_map/ppermute | solution.py:92
  390.8 14.1 %collective-permute-start.2 = (f32[4,64,256]{2,1,0:T(8,128)S(1)}, f32[4,64,256]{2,1,0:T(8,128)S(1)}, u32[]{:S(2)}, u32[]{:S(2)}) collective-permute-start(f32[4,64,256]{2,1,0:T(8,128)S(1)} %add.68), channel_id=1, source_target_pairs={{0,4},{1,5},{2,6},{3,7},{4,0},{5,1},{6,2},{7,3},{8,12},{9,13},{10,... | collective-permute-start | bytes 786440 | tf_op jit(solution)/shard_map/ppermute | solution.py:92
Sparse Core Ops, SparseCore 0:
  9.6 31.7 all-gather.1
  45.1 52.1 all-reduce.3
  269.4 45.3 all-reduce.5
  317.6 58.8 all-reduce.7
